TPU v7x, 32 devices: a whole 2x2x4 slice. The times are simulated.
32 devices in a mesh: seq: 4 (over y, core), wide: 8 (over z, x).
Axes of the slice: x: 2, y: 2, z: 4, core: 2. Of those that a mesh axis runs over, the one named last changes fastest.
Arguments:
- qkv_proj: bfloat16 [3, 2, 2048, 4096], P(None, None, ('seq', 'wide')), may hold values from -6 to 6
- conv_kernel: float32 [3, 4, 4096], replicated, may hold values from -3 to 3
- qk_gain: float32 [2, 8, 512], P(None, 'wide'), may hold values from 0.4 to 2.5
- fast_init: float32 [3, 8, 512, 512], P(None, 'wide'), may hold values from -0.25 to 0.25
- step_size: float32 [8], P('wide'), may hold values from 0.2 to 1
Outputs:
- fast_out: bfloat16 [2, 2048, 4096], P(None, 'seq', 'wide')
All inputs are finite; a program needn't handle non-finite values.
Results may differ from a plain program's by a relative error of at most 0.004.
Values may be sent and summed in bfloat16 or wider, within the bound.
A program may use at most 128 MiB of HBM per device.

v0:
```python
import jax
import jax.numpy as jnp
from jax import lax
from jax.sharding import PartitionSpec as P

HEAD = 512
GROUPS = 2
KW = 4


EPS = 1e-06
BETA = 0.6


def from_behind(value, axis, steps):
    count = lax.axis_size(axis)
    pairs = [(source, (source + steps) % count) for source in range(count)]
    return lax.ppermute(value, axis, pairs)


def matmul(left, right):
    return jnp.dot(left, right, preferred_element_type=jnp.float32)


def contract_rows(left, right):
    return lax.dot_general(
        left, right, (((0,), (0,)), ((), ())), preferred_element_type=jnp.float32
    )


def contract_cols(left, right):
    return lax.dot_general(
        left, right, (((1,), (1,)), ((), ())), preferred_element_type=jnp.float32
    )


def rms_rows(values_in):
    values_in = values_in.astype(jnp.float32)
    return values_in * lax.rsqrt(jnp.mean(values_in * values_in, axis=-1, keepdims=True) + EPS)


def normalize_columns(moment):
    return moment * lax.rsqrt(jnp.mean(moment * moment, axis=1, keepdims=True) + EPS)


def local_gradients(weights, keys_in, values_in):
    narrow = weights.astype(jnp.bfloat16)
    gate_pre = matmul(keys_in, narrow[0])
    up_pre = matmul(keys_in, narrow[1])
    sigmoid_gate = jax.nn.sigmoid(gate_pre)
    gate_act = gate_pre * sigmoid_gate
    hidden = (gate_act * up_pre).astype(jnp.bfloat16)
    back_hidden = contract_cols(values_in, narrow[2])
    g_down = contract_rows(hidden, values_in)
    err_gate = (
        back_hidden * up_pre * sigmoid_gate * (1.0 + gate_pre * (1.0 - sigmoid_gate))
    ).astype(jnp.bfloat16)
    err_up = (back_hidden * gate_act).astype(jnp.bfloat16)
    g_gate = contract_rows(keys_in, err_gate)
    g_up = contract_rows(keys_in, err_up)
    return jnp.stack([g_gate, g_up, g_down])


def apply_fast(weights, queries):
    narrow = weights.astype(jnp.bfloat16)
    hidden = (jax.nn.silu(matmul(queries, narrow[0])) * matmul(queries, narrow[1])).astype(
        jnp.bfloat16
    )
    return matmul(hidden, narrow[2])


def conv_rows(extended, kernel, row_count):
    rim_width = KW - 1
    summed = jnp.zeros(extended.shape[:2] + (row_count, extended.shape[3]), jnp.float32)
    for tap_index in range(KW):
        begin = rim_width - tap_index
        summed = summed + kernel[:, tap_index][:, None, None, :] * extended[
            :, :, begin : begin + row_count, :
        ].astype(jnp.float32)
    return summed


def local(qkv_proj, conv_kernel, qk_gain, fast_init, step_size):
    row_count = qkv_proj.shape[2]
    rim_width = KW - 1
    tail_rows = qkv_proj[:, :, row_count - rim_width :, :]
    before = from_behind(tail_rows, ("seq", "wide"), 1)
    shifted = jnp.concatenate([jnp.zeros_like(before[:, :1]), before[:, :-1]], axis=1)
    leading = lax.axis_index(("seq", "wide")) == 0
    rim_rows = jnp.where(leading, shifted, before)
    extended = jnp.concatenate([rim_rows, qkv_proj], axis=2)
    activated = jax.nn.silu(conv_rows(extended, conv_kernel, row_count)).astype(jnp.bfloat16)
    seq_count = lax.axis_size("seq")
    group_total = row_count * lax.axis_size("wide") * seq_count
    gains = qk_gain[:, 0]
    weights = fast_init[:, 0]
    step_scale = step_size[0] * HEAD ** (-0.5)
    momentum = None
    outputs = []
    for group_index in range(GROUPS):
        group_data = lax.all_to_all(
            activated[:, group_index], "wide", split_axis=2, concat_axis=1, tiled=True
        )
        queries = (rms_rows(group_data[0]) * gains[0]).astype(jnp.bfloat16)
        keys_in = (rms_rows(group_data[1]) * gains[1]).astype(jnp.bfloat16)
        values_in = group_data[2] * (-1.0 / group_total)
        gradients = local_gradients(weights, keys_in, values_in)
        summed = lax.psum(gradients.astype(jnp.bfloat16), "seq").astype(jnp.float32)
        if momentum is None:
            momentum = jnp.zeros_like(summed)
        momentum = BETA * momentum + summed
        weights = weights - step_scale * normalize_columns(momentum)
        outputs.append(apply_fast(weights, queries))
    return jnp.stack(outputs).astype(jnp.bfloat16)


def solution(mesh):
    in_specs = (
        P(None, None, ("seq", "wide"), None),
        P(),
        P(None, "wide", None),
        P(None, "wide", None, None),
        P("wide"),
    )
    out_specs = P(None, "seq", "wide")
    return jax.shard_map(local, mesh=mesh, in_specs=in_specs, out_specs=out_specs, check_vma=False)
```

profile of v0, /device:TPU:31, one launch (start us, length us, event | category | flops | bytes accessed | tf_op | source)
XLA Modules:
  0.0 261.4 jit_solution(11459366017224113789)
XLA Ops:
  7.9 1.5 fusion.61
  9.6 3.0 %collective-permute-done = bf16[3,2,3,4096]{3,1,2,0:T(2,128)(2,1)S(1)} collective-permute-done((bf16[3,2,3,4096]{3,1,2,0:T(2,128)(2,1)S(1)}, bf16[3,2,3,4096]{3,1,2,0:T(2,128)(2,1)S(1)}, u32[]{:S(2)}, u32[]{:S(2)}) %collective-permute-start) | collective-permute-done | bytes 147488 | tf_op jit(solution)/shard_map/ppermute | solution.py:18
  12.9 9.7 %multiply_convert_fusion = bf16[3,2,64,4096]{3,2,1,0:T(8,128)(2,1)S(1)} fusion(bf16[3,2,64,4096]{3,2,1,0:T(8,128)(2,1)} %param.5, bf16[3,2,3,4096]{3,2,1,0:T(4,128)(2,1)S(1)} %pad_select_fusion, f32[3,4096]{1,0:T(4,128)S(1)} %get-tuple-element.29, f32[3,4096]{1,0:T(4,128)S(1)} %get-tuple-element.30, f32[3,4096]{1,0:T(4,128)S(1)} %get-tuple-element.31, ...), kind=kLoop, calls=%fused_computation | loop fusion | flops 39321600 | bytes 6635520 | tf_op jit(solution)/shard_map/convert_element_type | solution.py:92
  22.6 2.1 slice_bitcast_fusion.1
  24.7 6.4 %copy.82 = bf16[3,64,4096]{1,0,2:T(4,128)(2,1)} copy(bf16[3,64,4096]{2,1,0:T(8,128)(2,1)} %get-tuple-element.9) | data formatting | bytes 3145728 | tf_op jit(solution)/shard_map/squeeze | solution.py:102
  31.1 7.4 %reshape.212 = bf16[8,2,49152]{2,1,0:T(2,128)(2,1)} reshape(bf16[4096,3,64]{2,1,0:T(4,128)(2,1)} %bitcast.113) | data formatting | bytes 3145728
  38.5 8.1 %all-to-all-start = ((bf16[8,2,49152]{2,1,0:T(2,128)(2,1)}), bf16[8,2,49152]{2,1,0:T(2,128)(2,1)}, u32[]{:S(2)}, u32[]{:S(2)}) async-start(bf16[8,2,49152]{2,1,0:T(2,128)(2,1)} %reshape.212), calls=%async_computation | async-start | bytes 3145728 | tf_op jit(solution)/shard_map/all_to_all | solution.py:101
  46.6 4.7 %copy.92 = bf16[3,64,4096]{1,0,2:T(4,128)(2,1)} copy(bf16[3,64,4096]{2,1,0:T(8,128)(2,1)S(1)} %copy-done.3) | data formatting | bytes 3145728 | tf_op jit(solution)/shard_map/squeeze | solution.py:102
  51.3 7.4 %reshape.210 = bf16[8,2,49152]{2,1,0:T(2,128)(2,1)} reshape(bf16[4096,3,64]{2,1,0:T(4,128)(2,1)} %bitcast.114) | data formatting | bytes 3145728
  58.7 23.4 %all-to-all-done = bf16[8,2,49152]{2,1,0:T(2,128)(2,1)} async-done(((bf16[8,2,49152]{2,1,0:T(2,128)(2,1)}), bf16[8,2,49152]{2,1,0:T(2,128)(2,1)}, u32[]{:S(2)}, u32[]{:S(2)}) %all-to-all-start) | async-done | bytes 1572896 | tf_op jit(solution)/shard_map/all_to_all | solution.py:101
  82.0 5.4 %all-to-all-start.1 = ((bf16[8,2,49152]{2,1,0:T(2,128)(2,1)}), bf16[8,2,49152]{2,1,0:T(2,128)(2,1)}, u32[]{:S(2)}, u32[]{:S(2)}) async-start(bf16[8,2,49152]{2,1,0:T(2,128)(2,1)} %reshape.210), calls=%async_computation.1 | async-start | bytes 3145728 | tf_op jit(solution)/shard_map/all_to_all | solution.py:101
  88.9 7.1 %reshape.213 = bf16[4096,3,64]{2,1,0:T(4,128)(2,1)} reshape(bf16[8,2,49152]{2,1,0:T(2,128)(2,1)} %all-to-all-done) | data formatting | bytes 3145728
  96.0 5.2 %copy.102 = bf16[3,64,8,512]{3,2,1,0:T(8,128)(2,1)} copy(bf16[3,64,8,512]{1,0,3,2:T(4,128)(2,1)} %bitcast.115) | data formatting | bytes 3145728 | tf_op jit(solution)/shard_map/all_to_all | solution.py:101
  101.2 1.5 fusion.17
  102.7 2.5 slice_convert_fusion.1
  105.2 17.8 %all-to-all-done.1 = bf16[8,2,49152]{2,1,0:T(2,128)(2,1)} async-done(((bf16[8,2,49152]{2,1,0:T(2,128)(2,1)}), bf16[8,2,49152]{2,1,0:T(2,128)(2,1)}, u32[]{:S(2)}, u32[]{:S(2)}) %all-to-all-start.1) | async-done | bytes 1572896 | tf_op jit(solution)/shard_map/all_to_all | solution.py:101
  123.0 7.1 %reshape.211 = bf16[4096,3,64]{2,1,0:T(4,128)(2,1)} reshape(bf16[8,2,49152]{2,1,0:T(2,128)(2,1)} %all-to-all-done.1) | data formatting | bytes 3145728
  130.1 5.3 %copy.103 = bf16[3,64,8,512]{3,2,1,0:T(8,128)(2,1)} copy(bf16[3,64,8,512]{1,0,3,2:T(4,128)(2,1)} %bitcast.116) | data formatting | bytes 3145728 | tf_op jit(solution)/shard_map/all_to_all | solution.py:101
  135.3 1.5 multiply_reduce_fusion.1
  136.8 2.5 slice_convert_fusion
  140.1 3.3 %multiply_convert_fusion.4 = (bf16[1,8,64,512]{3,1,2,0:T(8,128)(2,1)}, bf16[1,8,64,512]{3,1,2,0:T(8,128)(2,1)}, bf16[1,8,64,512]{3,1,2,0:T(8,128)(2,1)S(1)}, bf16[1,8,64,512]{3,1,2,0:T(8,128)(2,1)}) fusion(f32[8,64]{0,1:T(8,128)S(1)} %copy.100, f32[512]{0:T(512)S(1)} %bitcast.136, bf16[3,8,64,512]{3,1,2,0:T(8,128)(2,1)} %bitcast.122, f32[512]{0:T(512)S(1)} %bitcast.138, ...), kind=kLoop, calls=%fused_computation.70 | loop fusion | flops 4194304 | bytes 4206592 | tf_op jit(solution)/shard_map/convert_element_type | solution.py:105
  151.7 2.0 copy.99
  153.7 2.0 copy.101
  155.7 38.1 %all-reduce.4.cloned.1.call-done = bf16[3,512,512]{2,1,0:T(8,128)(2,1)} async-done(((bf16[3,512,512]{2,1,0:T(8,128)(2,1)}), bf16[3,512,512]{2,1,0:T(8,128)(2,1)}) %all-reduce.4.cloned.1.call-update) | async-done | bytes 1572880 | tf_op jit(solution)/shard_map/psum | solution.py:108
  193.8 1.7 fusion.2
  195.5 2.1 fusion.6
  203.9 2.2 copy.96
  206.1 2.5 fusion.46
  208.6 3.5 %fusion.9 = bf16[1,512,512]{2,1,0:T(8,128)(2,1)} fusion(bf16[512,512]{1,0:T(8,128)(2,1)} %bitcast.134, f32[512,512]{1,0:T(8,128)} %fusion.46, bf16[3,512,512]{2,1,0:T(8,128)(2,1)} %copy-done.2), kind=kOutput, calls=%fused_computation.39 | convolution fusion | flops 538705920 | bytes 3145728 | tf_op jit(solution)/shard_map/dot_general | solution.py:22
  212.1 33.7 %all-reduce.6.cloned.1.call-done = bf16[3,512,512]{2,1,0:T(8,128)(2,1)} async-done(((bf16[3,512,512]{2,1,0:T(8,128)(2,1)}), bf16[3,512,512]{2,1,0:T(8,128)(2,1)}) %all-reduce.6.cloned.1.call-update) | async-done | bytes 1572880 | tf_op jit(solution)/shard_map/psum | solution.py:108
  245.8 2.7 %multiply_reduce_fusion = f32[3,512]{1,0:T(4,128)S(1)} fusion(bf16[3,512,512]{2,1,0:T(8,128)(2,1)} %all-reduce.6.cloned.1.call-done, bf16[3,512,512]{2,1,0:T(8,128)(2,1)} %all-reduce.4.cloned.1.call-done), kind=kLoop, calls=%fused_computation.17 | loop fusion | flops 4717056 | bytes 3151872 | tf_op jit(solution)/shard_map/reduce_sum | solution.py:43
  251.3 2.2 fusion.10
  (86 shorter events, 21.7 us)
Async XLA Ops:
  7.8 4.8 %collective-permute-start = (bf16[3,2,3,4096]{3,1,2,0:T(2,128)(2,1)S(1)}, bf16[3,2,3,4096]{3,1,2,0:T(2,128)(2,1)S(1)}, u32[]{:S(2)}, u32[]{:S(2)}) collective-permute-start(bf16[3,2,3,4096]{3,1,2,0:T(2,128)(2,1)S(1)} %copy.108), channel_id=1, source_target_pairs={{0,1},{1,2},{2,3},{3,4},{4,5},{5,6},{6,7},{7,8},{8,9},{9,10},{10,1... | collective-permute-start | bytes 442376 | tf_op jit(solution)/shard_map/ppermute | solution.py:18
  31.1 15.5 %copy-start.3 = (bf16[3,64,4096]{2,1,0:T(8,128)(2,1)S(1)}, bf16[3,64,4096]{2,1,0:T(8,128)(2,1)}, u32[]{:S(2)}) copy-start(bf16[3,64,4096]{2,1,0:T(8,128)(2,1)} %get-tuple-element.10) | copy-start | bytes 4718596
  38.5 43.5 %all-to-all-start = ((bf16[8,2,49152]{2,1,0:T(2,128)(2,1)}), bf16[8,2,49152]{2,1,0:T(2,128)(2,1)}, u32[]{:S(2)}, u32[]{:S(2)}) async-start(bf16[8,2,49152]{2,1,0:T(2,128)(2,1)} %reshape.212), calls=%async_computation | async-start | bytes 3145728 | tf_op jit(solution)/shard_map/all_to_all | solution.py:101
  51.3 36.2 %copy-start.16 = (f32[2,1,512]{2,1,0:T(1,128)S(1)}, f32[2,1,512]{2,1,0:T(1,128)}, u32[]{:S(2)}) copy-start(f32[2,1,512]{2,1,0:T(1,128)} %param.7) | copy-start | bytes 12292
  51.3 36.2 %copy-start = (f32[3,1,512,512]{3,2,1,0:T(8,128)S(1)}, f32[3,1,512,512]{3,2,1,0:T(8,128)}, u32[]{:S(2)}) copy-start(f32[3,1,512,512]{3,2,1,0:T(8,128)} %param.8) | copy-start | bytes 9437188
  82.0 40.9 %all-to-all-start.1 = ((bf16[8,2,49152]{2,1,0:T(2,128)(2,1)}), bf16[8,2,49152]{2,1,0:T(2,128)(2,1)}, u32[]{:S(2)}, u32[]{:S(2)}) async-start(bf16[8,2,49152]{2,1,0:T(2,128)(2,1)} %reshape.210), calls=%async_computation.1 | async-start | bytes 3145728 | tf_op jit(solution)/shard_map/all_to_all | solution.py:101
  87.5 106.3 %all-reduce.4.cloned.1.call-start = ((), (), s32[]{:S(2)}) async-start(), calls=%async_computation.2 | async-start | bytes 3145728 | tf_op jit(solution)/shard_map/psum | solution.py:108
  140.1 3.5 %copy-start.4 = (bf16[3,512,512]{2,1,0:T(8,128)(2,1)S(1)}, bf16[3,512,512]{2,1,0:T(8,128)(2,1)}, u32[]{:S(2)}) copy-start(bf16[3,512,512]{2,1,0:T(8,128)(2,1)} %bitcast_convert_fusion) | copy-start | bytes 4718596
  143.4 1.2 copy-start.7
  143.6 1.7 copy-start.8
  144.0 1.8 copy-start.10
  150.8 95.0 %all-reduce.6.cloned.1.call-start = ((), (), s32[]{:S(2)}) async-start(), calls=%async_computation.3 | async-start | bytes 3145728 | tf_op jit(solution)/shard_map/psum | solution.py:108
  195.5 2.1 copy-start.6
  197.6 1.9 copy-start.2
  197.6 1.4 copy-start.11
  197.6 1.9 copy-start.14
  203.9 2.2 copy-start.13
  245.8 2.7 %copy-start.1 = (bf16[3,512,512]{2,1,0:T(8,128)(2,1)S(1)}, bf16[3,512,512]{2,1,0:T(8,128)(2,1)}, u32[]{:S(2)}) copy-start(bf16[3,512,512]{2,1,0:T(8,128)(2,1)} %all-reduce.4.cloned.1.call-done) | copy-start | bytes 4718596
  245.8 2.8 %copy-start.5 = (bf16[3,512,512]{2,1,0:T(8,128)(2,1)S(1)}, bf16[3,512,512]{2,1,0:T(8,128)(2,1)}, u32[]{:S(2)}) copy-start(bf16[3,512,512]{2,1,0:T(8,128)(2,1)} %all-reduce.6.cloned.1.call-done) | copy-start | bytes 4718596
  248.6 2.3 copy-start.12
  249.7 1.2 copy-start.9
  251.3 2.2 copy-start.15
Sparse Core Ops, SparseCore 0:
  150.9 42.8 all-reduce.3
  202.8 42.8 all-reduce.5
where the time goes:
time: 266 us; the launch traced here: 261 us
  waiting for transfers between devices  116 us (44%)
  local copies, waits for them, and re-layouts  67.4 us (25%)
  other arithmetic  34.9 us (13%)
  matrix products  14.9 us (6%)
  between operations  14.4 us (5%)
  starting transfers between devices  13.8 us (5%)
    psum x2, waiting for transfers between devices, local(): summed = lax.psum(gradients.astype(jnp.bfloat16), 'seq').astype(jnp.float32)  71.8 us
    all_to_all x2, waiting for transfers between devices, local(): lax.all_to_all(activated[:, group_index], 'wide', split_axis=2, concat_ax...  41.2 us
    unnamed x42, local copies, waits for them, and re-layouts  31.4 us
    all_to_all x2, starting transfers between devices, local(): lax.all_to_all(activated[:, group_index], 'wide', split_axis=2, concat_ax...  13.5 us
    squeeze x3, local copies, waits for them, and re-layouts, local(): activated[:, group_index]  13.1 us
    all_to_all x2, local copies, waits for them, and re-layouts, local(): lax.all_to_all(activated[:, group_index], 'wide', split_axis=2, concat_ax...  10.5 us
    dot_general x8, matrix products, matmul(): return jnp.dot(left, right, preferred_element_type=jnp.float32)  10.3 us
    convert_element_type x1, other arithmetic, local(): jax.nn.silu(conv_rows(extended, conv_kernel, row_count))  9.74 us
  transfers between devices with their start and end apart: 5, of which 5 were waited for; matrix products, arithmetic and copies ran while one was open for 17% of the time, Pallas kernels for 0%

commit v1 on v0

v1 whole, which is shorter than its diff:
```python
import functools

import jax
import jax.numpy as jnp
from jax import lax
from jax.experimental import pallas as pl
from jax.experimental.pallas import tpu as pltpu
from jax.sharding import PartitionSpec as P

EPS = 1e-06
BETA = 0.6
RIM = 16
MESH = pl.DeviceIdType.MESH


def dot(left, right, left_dim=1, right_dim=0):
    return lax.dot_general(
        left,
        right,
        (((left_dim,), (right_dim,)), ((), ())),
        preferred_element_type=jnp.float32,
    )


def sigmoid(v):
    return 0.5 * jnp.tanh(0.5 * v) + 0.5


def silu(v):
    half = 0.5 * v
    return half * jnp.tanh(half) + half


def rms(v, gain):
    v = v.astype(jnp.float32)
    scale = lax.rsqrt(jnp.mean(v * v, axis=-1, keepdims=True) + EPS)
    return (v * scale * gain).astype(jnp.bfloat16)


def kernel(
    seq_count,
    wide_count,
    qkv,
    taps_ref,
    gain_ref,
    init_ref,
    step_ref,
    out_ref,
    raw,
    keys,
    values,
    queries,
    mids,
    weights,
    narrow,
    moment,
    pair_out,
    pair_in,
    half_sum,
    chip_out,
    chip_in,
    a2a_send,
    a2a_recv,
    rim_send,
    rim_recv,
    pair_send,
    pair_recv,
    chip_send,
    chip_recv,
    wide_send,
    wide_recv,
    init_sem,
):
    group_count, row_count = qkv.shape[1], qkv.shape[2]
    tap_count = taps_ref.shape[1]
    head = init_ref.shape[-1]
    half = head // 2
    tokens = row_count * wide_count
    group_total = tokens * seq_count
    chip_count = seq_count // 2
    seq, wide = lax.axis_index("seq"), lax.axis_index("wide")
    core, chip = lax.rem(seq, 2), seq // 2
    partner = 2 * chip + (1 - core)
    block = min(256, tokens)

    barrier = pltpu.get_barrier_semaphore()
    for d in range(1, wide_count):
        pl.semaphore_signal(
            barrier, inc=1, device_id=(seq, lax.rem(wide + d, wide_count)), device_id_type=MESH
        )
    for d in range(1, seq_count):
        pl.semaphore_signal(
            barrier, inc=1, device_id=(lax.rem(seq + d, seq_count), wide), device_id_type=MESH
        )
    pl.semaphore_wait(barrier, wide_count + seq_count - 2)

    phases = [(1, 2, g) for g in range(group_count)] + [(0, 1, g) for g in range(group_count)]

    def head_cols(h):
        return pl.ds(pl.multiple_of(h * head, head), head)

    def chunk_rows(w):
        return pl.ds(pl.multiple_of(RIM + w * row_count, RIM), row_count)

    def regroup_copy(phase, d):
        first, count, g = phases[phase]
        target = lax.rem(wide + d, wide_count)
        return pltpu.make_async_remote_copy(
            src_ref=qkv.at[pl.ds(first, count), g, :, head_cols(target)],
            dst_ref=raw.at[pl.ds(first, count), g, chunk_rows(wide), :],
            send_sem=a2a_send.at[phase, d],
            recv_sem=a2a_recv.at[phase, wide],
            device_id=(seq, target),
            device_id_type=MESH,
        )

    def start_regroup(phase):
        first, count, g = phases[phase]
        for d in range(1, wide_count):
            regroup_copy(phase, d).start()
        pltpu.make_async_copy(
            qkv.at[pl.ds(first, count), g, :, head_cols(wide)],
            raw.at[pl.ds(first, count), g, chunk_rows(wide), :],
            a2a_recv.at[phase, wide],
        ).start()

    def end_regroup(phase):
        for d in range(1, wide_count):
            regroup_copy(phase, d).wait_send()

    def wait_chunk(phase, w):
        first, count, g = phases[phase]
        pltpu.make_async_copy(
            qkv.at[pl.ds(first, count), g, :, head_cols(wide)],
            raw.at[pl.ds(first, count), g, chunk_rows(w), :],
            a2a_recv.at[phase, w],
        ).wait()

    def rim_copy(phase):
        first, count, g = phases[phase]
        wraps = (seq + 1) // seq_count
        to_group = jnp.minimum(g + wraps, group_count - 1)
        return pltpu.make_async_remote_copy(
            src_ref=raw.at[pl.ds(first, count), g, pl.ds(tokens, RIM), :],
            dst_ref=raw.at[pl.ds(first, count), to_group, pl.ds(0, RIM), :],
            send_sem=rim_send.at[phase],
            recv_sem=rim_recv.at[phase - g + to_group],
            device_id=(lax.rem(seq + 1, seq_count), wide),
            device_id_type=MESH,
        )

    def wait_rim(phase):
        first, count, g = phases[phase]
        pltpu.make_async_copy(
            raw.at[pl.ds(first, count), g, pl.ds(tokens, RIM), :],
            raw.at[pl.ds(first, count), g, pl.ds(0, RIM), :],
            rim_recv.at[phase],
        ).wait()

    def rim_sends(phase, act):
        if phases[phase][2] == group_count - 1:
            pl.when(seq < seq_count - 1)(act)
        else:
            act()

    def conv_chunk(phase, w):
        first, count, g = phases[phase]
        base = pl.multiple_of(w * row_count, RIM)
        for stream in range(first, first + count):
            rows = raw[stream, g, pl.ds(base, RIM + row_count), :].astype(jnp.float32)
            taps = taps_ref[stream, :, head_cols(wide)]
            summed = taps[0:1] * rows[RIM : RIM + row_count]
            for j in range(1, tap_count):
                summed = summed + taps[j : j + 1] * rows[RIM - j : RIM - j + row_count]
            activated = silu(summed).astype(jnp.bfloat16)
            at = pl.ds(base, row_count)
            if stream == 0:
                queries[at, :] = rms(activated, gain_ref[0])
            elif stream == 1:
                keys[at, :] = rms(activated, gain_ref[1])
            else:
                values[at, :] = (activated.astype(jnp.float32) * (-1.0 / group_total)).astype(
                    jnp.bfloat16
                )

    def convolve(phase):
        wait_chunk(phase, 0)
        wait_chunk(phase, wide_count - 1)
        rim_sends(phase, lambda: rim_copy(phase).start())

        def body(w, carry):
            wait_chunk(phase, w)
            conv_chunk(phase, w)
            return carry

        lax.fori_loop(1, wide_count - 1, body, 0)
        conv_chunk(phase, wide_count - 1)
        if phases[phase][2] == 0:
            pl.when(seq > 0)(lambda: wait_rim(phase))
        else:
            wait_rim(phase)
        conv_chunk(phase, 0)

    def pair_copy(g, m):
        return pltpu.make_async_remote_copy(
            src_ref=pair_out.at[g, m],
            dst_ref=pair_in.at[g, m],
            send_sem=pair_send.at[g, m],
            recv_sem=pair_recv.at[g, m],
            device_id=(partner, wide),
            device_id_type=MESH,
        )

    def chip_copy(g, m, d):
        other = 2 * lax.rem(chip + d, chip_count) + core
        return pltpu.make_async_remote_copy(
            src_ref=chip_out.at[g, m],
            dst_ref=chip_in.at[g, m, d - 1],
            send_sem=chip_send.at[g, m, d - 1],
            recv_sem=chip_recv.at[g, m, d - 1],
            device_id=(other, wide),
            device_id_type=MESH,
        )

    own_cols = pl.ds(pl.multiple_of(core * half, half), half)
    other_cols = pl.ds(pl.multiple_of((1 - core) * half, half), half)

    def weight_copy(g, m, cols):
        return pltpu.make_async_remote_copy(
            src_ref=narrow.at[g + 1, m, :, cols],
            dst_ref=narrow.at[g + 1, m, :, cols],
            send_sem=wide_send.at[g, m],
            recv_sem=wide_recv.at[g, m],
            device_id=(partner, wide),
            device_id_type=MESH,
        )

    def gradients(g):
        for t in range(tokens // block):
            at = pl.ds(t * block, block)
            a = dot(keys[at, :], narrow[g, 0])
            b = dot(keys[at, :], narrow[g, 1])
            sg = sigmoid(a)
            act = a * sg
            mids[2, at, :] = (act * b).astype(jnp.bfloat16)
            back = dot(values[at, :], narrow[g, 2], 1, 1)
            mids[0, at, :] = (back * b * sg * (1.0 + a * (1.0 - sg))).astype(jnp.bfloat16)
            mids[1, at, :] = (back * act).astype(jnp.bfloat16)

        def part(m, cols):
            if m == 2:
                return dot(mids[2], values[:, cols], 0, 0)
            return dot(keys[...], mids[m, :, cols], 0, 0)

        for m in (2, 0, 1):
            pair_out[g, m] = part(m, other_cols).astype(jnp.bfloat16)
            pair_copy(g, m).start()
        for m in (2, 0, 1):
            half_sum[m] = part(m, own_cols)
            pair_copy(g, m).wait_recv()
            total = half_sum[m] + pair_in[g, m].astype(jnp.float32)
            half_sum[m] = total
            if chip_count > 1:
                chip_out[g, m] = total.astype(jnp.bfloat16)
                for d in range(1, chip_count):
                    chip_copy(g, m, d).start()

    def update(g):
        scale = step_ref[...] * head ** (-0.5)
        for m in (2, 0, 1):
            total = half_sum[m]
            for d in range(1, chip_count):
                chip_copy(g, m, d).wait_recv()
                total = total + chip_in[g, m, d - 1].astype(jnp.float32)
            if g > 0:
                total = BETA * moment[m] + total
            moment[m] = total
            norm = lax.rsqrt(jnp.mean(total * total, axis=0, keepdims=True) + EPS)
            new = weights[m, :, own_cols] - scale * (total * norm)
            weights[m, :, own_cols] = new
            narrow[g + 1, m, :, own_cols] = new.astype(jnp.bfloat16)
            weight_copy(g, m, own_cols).start()
        for m in (2, 0, 1):
            weight_copy(g, m, other_cols).wait_recv()

    def apply(g):
        for t in range(tokens // block):
            at = pl.ds(t * block, block)
            a = dot(queries[at, :], narrow[g + 1, 0])
            b = dot(queries[at, :], narrow[g + 1, 1])
            p = (silu(a) * b).astype(jnp.bfloat16)
            out_ref[g, at, :] = dot(p, narrow[g + 1, 2]).astype(jnp.bfloat16)

    load = pltpu.make_async_copy(init_ref.at[:, 0], weights, init_sem)
    start_regroup(0)
    load.start()

    @pl.when(seq == 0)
    def _():
        for stream in range(3):
            raw[stream, 0, 0:RIM, :] = jnp.zeros((RIM, head), jnp.bfloat16)

    load.wait()
    for m in range(3):
        narrow[0, m] = weights[m].astype(jnp.bfloat16)

    for g in range(group_count):
        convolve(g)
        end_regroup(g)
        if g + 1 < group_count:
            start_regroup(g + 1)
        else:
            for later in range(group_count):
                start_regroup(group_count + later)
        if g > 0:
            update(g - 1)
        gradients(g)
    for g in range(group_count):
        convolve(group_count + g)
        if g == group_count - 1:
            update(g)
        apply(g)

    for phase in range(2 * group_count):
        if phase >= group_count:
            end_regroup(phase)
        rim_sends(phase, lambda phase=phase: rim_copy(phase).wait_send())
    for g in range(group_count):
        for m in range(3):
            pair_copy(g, m).wait_send()
            weight_copy(g, m, own_cols).wait_send()
            for d in range(1, chip_count):
                chip_copy(g, m, d).wait_send()


def local(qkv_proj, conv_kernel, qk_gain, fast_init, step_size):
    seq_count, wide_count = lax.axis_size("seq"), lax.axis_size("wide")
    group_count, row_count = qkv_proj.shape[1:3]
    head = fast_init.shape[-1]
    half = head // 2
    tokens = row_count * wide_count
    chip_slots = max(1, seq_count // 2 - 1)
    wide_type, full_type = jnp.bfloat16, jnp.float32
    vmem = pl.BlockSpec(memory_space=pltpu.VMEM)
    hbm = pl.BlockSpec(memory_space=pl.ANY)
    dma = pltpu.SemaphoreType.DMA
    matmuls = group_count * 9
    return pl.pallas_call(
        functools.partial(kernel, seq_count, wide_count),
        out_shape=jax.ShapeDtypeStruct((group_count, tokens, head), wide_type),
        in_specs=[hbm, vmem, vmem, hbm, vmem],
        out_specs=vmem,
        scratch_shapes=[
            pltpu.VMEM((3, group_count, RIM + tokens, head), wide_type),
            pltpu.VMEM((tokens, head), wide_type),
            pltpu.VMEM((tokens, head), wide_type),
            pltpu.VMEM((tokens, head), wide_type),
            pltpu.VMEM((3, tokens, head), wide_type),
            pltpu.VMEM((3, head, head), full_type),
            pltpu.VMEM((group_count + 1, 3, head, head), wide_type),
            pltpu.VMEM((3, head, half), full_type),
            pltpu.VMEM((group_count, 3, head, half), wide_type),
            pltpu.VMEM((group_count, 3, head, half), wide_type),
            pltpu.VMEM((3, head, half), full_type),
            pltpu.VMEM((group_count, 3, head, half), wide_type),
            pltpu.VMEM((group_count, 3, chip_slots, head, half), wide_type),
            dma((2 * group_count, wide_count)),
            dma((2 * group_count, wide_count)),
            dma((2 * group_count,)),
            dma((2 * group_count,)),
            dma((group_count, 3)),
            dma((group_count, 3)),
            dma((group_count, 3, chip_slots)),
            dma((group_count, 3, chip_slots)),
            dma((group_count, 3)),
            dma((group_count, 3)),
            dma(()),
        ],
        compiler_params=pltpu.CompilerParams(
            collective_id=0, has_side_effects=True, vmem_limit_bytes=56 * 1024 * 1024
        ),
        cost_estimate=pl.CostEstimate(
            flops=matmuls * 2 * tokens * head * head,
            bytes_accessed=2 * qkv_proj.size,
            transcendentals=qkv_proj.size,
        ),
    )(qkv_proj, conv_kernel, qk_gain, fast_init, step_size.reshape(1, 1))


def solution(mesh):
    in_specs = (
        P(None, None, ("seq", "wide"), None),
        P(),
        P(None, "wide", None),
        P(None, "wide", None, None),
        P("wide"),
    )
    out_specs = P(None, "seq", "wide")
    return jax.shard_map(local, mesh=mesh, in_specs=in_specs, out_specs=out_specs, check_vma=False)
```

time: 266 us -> 98.4 us (0.37); the launches traced: 261 us -> 98.2 us
  waiting for transfers between devices: 116 us -> 0 us
  Pallas kernels: 0 us -> 95.3 us
  local copies, waits for them, and re-layouts: 67.4 us -> 2.26 us
  other arithmetic: 34.9 us -> 0 us
  matrix products: 14.9 us -> 0 us
  starting transfers between devices: 13.8 us -> 0 us
  between operations: 14.4 us -> 0.66 us
    pallas_call x0 -> x1, Pallas kernels: none -> 95.3 us  [local(): pl.pallas_call(functools.partial(kernel, seq_count, wide_count), out_shap...]
    psum x2 -> x0, waiting for transfers between devices: 71.8 us -> none  [local(): summed = lax.psum(gradients.astype(jnp.bfloat16), 'seq').astype(jnp.float32)]
    all_to_all x2 -> x0, waiting for transfers between devices: 41.2 us -> none  [local(): lax.all_to_all(activated[:, group_index], 'wide', split_axis=2, concat_ax...]
    unnamed x42 -> x1, local copies, waits for them, and re-layouts: 31.4 us -> 2.26 us
    convert_element_type x8 -> x0, other arithmetic: 23.6 us -> none  [the longest x1 9.74 us: local(): jax.nn.silu(conv_rows(extended, conv_kernel, row_count))]
    dot_general x16 -> x0, matrix products: 14.9 us -> none  [the longest x8 10.3 us: matmul(): return jnp.dot(left, right, preferred_element_type=jnp.float32)]
    all_to_all x2 -> x0, starting transfers between devices: 13.5 us -> none  [local(): lax.all_to_all(activated[:, group_index], 'wide', split_axis=2, concat_ax...]
    squeeze x3 -> x0, local copies, waits for them, and re-layouts: 13.1 us -> none  [local(): activated[:, group_index]]
  transfers between devices with their start and end apart: 5 -> 0, of which waited for: 5 -> 0; matrix products, arithmetic and copies ran while one was open for 17% -> 0% of each run, Pallas kernels for 0% -> 0%
where the time goes in v1:
time: 98.4 us; the launch traced here: 98.2 us
  Pallas kernels  95.3 us (97%)
  local copies, waits for them, and re-layouts  2.26 us (2%)
    pallas_call x1, Pallas kernels, local(): pl.pallas_call(functools.partial(kernel, seq_count, wide_count), out_shap...  95.3 us
    unnamed x1, local copies, waits for them, and re-layouts  2.26 us

profile of v1, /device:TPU:31, one launch (start us, length us, event | category | flops | bytes accessed | tf_op | source)
XLA Modules:
  0.0 98.2 jit_solution(2054379501224151334)
XLA Ops:
  0.7 95.3 %shard_map.55 = bf16[2,512,512]{2,1,0:T(8,128)(2,1)} custom-call(bf16[3,2,64,4096]{3,2,1,0:T(8,128)(2,1)} %qkv.1, f32[3,4,4096]{2,1,0:T(4,128)} %taps_ref.1, f32[2,1,512]{2,1,0:T(1,128)} %gain_ref.1, f32[3,1,512,512]{3,2,1,0:T(8,128)} %init_ref.1, f32[1,1]{1,0:T(1,128)} %bitcast.1.step_ref), custom_call_target="tpu_custom_call" | custom-call | flops 4831838208 | bytes 3145728 | tf_op jit(solution)/shard_map/pallas_call | solution.py:348
  96.0 2.3 %copy.8 = bf16[2,512,512]{2,1,0:T(8,128)(2,1)} copy(bf16[2,512,512]{2,1,0:T(8,128)(2,1)} %shard_map.55) | data formatting | bytes 2097152

commit v2 on v1

--- a/solution.py
+++ b/solution.py
@@ -305,13 +305,13 @@
         narrow[0, m] = weights[m].astype(jnp.bfloat16)
 
     for g in range(group_count):
-        convolve(g)
         end_regroup(g)
         if g + 1 < group_count:
             start_regroup(g + 1)
         else:
             for later in range(group_count):
                 start_regroup(group_count + later)
+        convolve(g)
         if g > 0:
             update(g - 1)
         gradients(g)

time: 98.4 us -> 99.7 us (1.013)
  Pallas kernels: 95.3 us -> 96.6 us
    pallas_call x1, Pallas kernels: 95.3 us -> 96.6 us  [local(): pl.pallas_call(functools.partial(kernel, seq_count, wide_count), out_shap...]
where the time goes in v2:
time: 99.7 us; the launch traced here: 99.5 us
  Pallas kernels  96.6 us (97%)
  local copies, waits for them, and re-layouts  2.26 us (2%)
    pallas_call x1, Pallas kernels, local(): pl.pallas_call(functools.partial(kernel, seq_count, wide_count), out_shap...  96.6 us
    unnamed x1, local copies, waits for them, and re-layouts  2.26 us

profile of v2, /device:TPU:31, one launch (start us, length us, event | category | flops | bytes accessed | tf_op | source)
XLA Modules:
  0.0 99.5 jit_solution(11514146629685268)
XLA Ops:
  0.7 96.6 %shard_map.55 = bf16[2,512,512]{2,1,0:T(8,128)(2,1)} custom-call(bf16[3,2,64,4096]{3,2,1,0:T(8,128)(2,1)} %qkv.1, f32[3,4,4096]{2,1,0:T(4,128)} %taps_ref.1, f32[2,1,512]{2,1,0:T(1,128)} %gain_ref.1, f32[3,1,512,512]{3,2,1,0:T(8,128)} %init_ref.1, f32[1,1]{1,0:T(1,128)} %bitcast.1.step_ref), custom_call_target="tpu_custom_call" | custom-call | flops 4831838208 | bytes 3145728 | tf_op jit(solution)/shard_map/pallas_call | solution.py:348
  97.2 2.3 %copy.8 = bf16[2,512,512]{2,1,0:T(8,128)(2,1)} copy(bf16[2,512,512]{2,1,0:T(8,128)(2,1)} %shard_map.55) | data formatting | bytes 2097152

commit v3 on v1

--- a/solution.py
+++ b/solution.py
@@ -116,7 +116,7 @@
 
     def start_regroup(phase):
         first, count, g = phases[phase]
-        for d in range(1, wide_count):
+        for d in sorted(range(1, wide_count), key=lambda d: abs(d - wide_count // 2)):
             regroup_copy(phase, d).start()
         pltpu.make_async_copy(
             qkv.at[pl.ds(first, count), g, :, head_cols(wide)],

time: 98.4 us -> 96.9 us (0.985)
  the two profiles are of different devices: /device:TPU:31 before, /device:TPU:15 now
where the time goes in v3:
time: 96.9 us; the launch traced here: 96.7 us
  Pallas kernels  93.8 us (97%)
  local copies, waits for them, and re-layouts  2.26 us (2%)
    pallas_call x1, Pallas kernels, local(): pl.pallas_call(functools.partial(kernel, seq_count, wide_count), out_shap...  93.8 us
    unnamed x1, local copies, waits for them, and re-layouts  2.26 us

profile of v3, /device:TPU:15, one launch (start us, length us, event | category | flops | bytes accessed | tf_op | source)
XLA Modules:
  0.0 96.7 jit_solution(3570767530802612218)
XLA Ops:
  0.7 93.8 %shard_map.55 = bf16[2,512,512]{2,1,0:T(8,128)(2,1)} custom-call(bf16[3,2,64,4096]{3,2,1,0:T(8,128)(2,1)} %qkv.1, f32[3,4,4096]{2,1,0:T(4,128)} %taps_ref.1, f32[2,1,512]{2,1,0:T(1,128)} %gain_ref.1, f32[3,1,512,512]{3,2,1,0:T(8,128)} %init_ref.1, f32[1,1]{1,0:T(1,128)} %bitcast.1.step_ref), custom_call_target="tpu_custom_call" | custom-call | flops 4831838208 | bytes 3145728 | tf_op jit(solution)/shard_map/pallas_call | solution.py:348
  94.4 2.3 %copy.8 = bf16[2,512,512]{2,1,0:T(8,128)(2,1)} copy(bf16[2,512,512]{2,1,0:T(8,128)(2,1)} %shard_map.55) | data formatting | bytes 2097152
